TPU v7x, 512 devices: a whole 4x8x8 slice. The times are simulated.
512 devices in a mesh: dp: 16 (over y, core), rule: 32 (over x, z).
Axes of the slice: x: 4, y: 8, z: 8, core: 2. Of those that a mesh axis runs over, the one named last changes fastest.
Arguments:
- hidden_states: bfloat16 [4096, 8192], P(('dp', 'rule')), may hold values from -6 to 6
- attn_input: bfloat16 [4096, 8192], P(('dp', 'rule')), may hold values from -6 to 6
- rule_ids: int32 [4096, 2], replicated, may hold values from 0 to 127, as said below
- slot_ids: int32 [4096, 2], replicated, may hold values from -1 to 127, as said below
- cotangent: bfloat16 [4096, 2], replicated, may hold values from -6 to 6
- adapter_in: bfloat16 [128, 8192, 512], P('dp', 'rule'), may hold values from -0.0625 to 0.0625
- adapter_bias: float32 [128, 512], P('dp'), may hold values from -3 to 3
- adapter_out: float32 [128, 512], P('dp'), may hold values from -0.25 to 0.25
Outputs:
- rewards: bfloat16 [4096, 2], P('dp')
- adapter_in_grad: bfloat16 [128, 8192, 512], P('dp', 'rule')
- adapter_bias_grad: float32 [128, 512], P('dp')
- adapter_out_grad: float32 [128, 512], P('dp')
- o_proj_grad: bfloat16 [8192, 8192], P('rule', 'dp')
Inputs may be any that keep to these rules, and one draw needn't show every extreme that they name: `rule_ids`: the owner of rule r is r // 8. Among the 16 pairs of one block of 8 consecutive tokens at most 2 name rules of any one owner, and in every block some owner gets exactly 2. The two rules of a token differ. slot_ids[t, k] counts the earlier pairs, in the order of t then k, that name the same rule; it is -1 where that count reaches 128. Some rule fills all 128 rows.
All inputs are finite; a program needn't handle non-finite values.
Results may differ from a plain program's by a relative error of at most 0.03.
Values may be sent and summed in bfloat16 or wider, within the bound.
No kernel may reach another device: no remote copies, remote signals or barrier semaphores. Data moves between devices by JAX's collectives and lax.ppermute only.
A program may use at most 64 MiB of HBM per device.

v0:
```python
import jax
import jax.numpy as jnp
from jax import lax
from jax.sharding import PartitionSpec as P


def local(
    hidden_states, attn_input, rule_ids, slot_ids, cotangent, adapter_in, adapter_bias, adapter_out
):
    dp_size = lax.axis_size("dp")
    rule_size = lax.axis_size("rule")
    dp_index = lax.axis_index("dp")
    rule_index = lax.axis_index("rule")
    rows_dev = hidden_states.shape[0]
    adapters, feature_cols, hidden_units = adapter_in.shape
    send_cap = max(2, 4 * rows_dev // dp_size)
    capacity = 4 * rows_dev * rule_size // adapters
    block_count = dp_size * rule_size
    pair_count = 2 * rows_dev
    slot_count = dp_size * send_cap
    recv_count = slot_count * rule_size
    buffer_rows = adapters * capacity
    rule_all = rule_ids.reshape(block_count, pair_count)
    slot_all = slot_ids.reshape(block_count, pair_count)
    cot_all = cotangent.reshape(block_count, pair_count).astype(jnp.float32)
    owner_all = rule_all // adapters
    earlier = jnp.arange(pair_count)[None, :] < jnp.arange(pair_count)[:, None]
    same_owner = owner_all[:, :, None] == owner_all[:, None, :]
    rank_all = jnp.sum((same_owner & earlier[None]).astype(jnp.int32), axis=2)
    my_block = dp_index * rule_size + rule_index
    my_owner = lax.dynamic_index_in_dim(owner_all, my_block, 0, keepdims=False)
    my_rank = lax.dynamic_index_in_dim(rank_all, my_block, 0, keepdims=False)
    target = my_owner * send_cap + my_rank
    select_pairs = (jnp.arange(slot_count)[:, None] == target[None, :]).astype(jnp.int32)
    select_tokens = jnp.sum(select_pairs.reshape(slot_count, rows_dev, 2), axis=2).astype(
        jnp.bfloat16
    )
    outgoing = jnp.dot(select_tokens, hidden_states, preferred_element_type=jnp.float32).astype(
        jnp.bfloat16
    )
    outgoing = outgoing.reshape(dp_size, send_cap, rule_size, feature_cols)
    incoming = lax.all_to_all(
        lax.all_to_all(outgoing, "dp", split_axis=0, concat_axis=0, tiled=True),
        "rule",
        split_axis=2,
        concat_axis=2,
        tiled=True,
    )
    flat_in = jnp.concatenate(
        [incoming.reshape(recv_count, feature_cols), jnp.zeros((1, feature_cols), jnp.bfloat16)],
        axis=0,
    )
    block_dp = (jnp.arange(block_count) // rule_size)[:, None]
    block_rule = (jnp.arange(block_count) % rule_size)[:, None]
    recv_index = (block_dp * send_cap + rank_all) * rule_size + block_rule
    owned = (owner_all == dp_index) & (slot_all >= 0)
    buffer_pos = rule_all % adapters * capacity + slot_all
    pos_target = jnp.where(owned, buffer_pos, buffer_rows).reshape(-1)
    recv_target = jnp.where(owned, recv_index, recv_count).reshape(-1)
    to_recv = (
        jnp.full((buffer_rows + 1,), recv_count, jnp.int32)
        .at[pos_target]
        .set(recv_index.reshape(-1))[:buffer_rows]
    )
    to_buffer = (
        jnp.full((recv_count + 1,), buffer_rows, jnp.int32)
        .at[recv_target]
        .set(buffer_pos.reshape(-1))[:recv_count]
    )
    cot_buffer = (
        jnp.zeros((buffer_rows + 1,), jnp.float32)
        .at[pos_target]
        .set(cot_all.reshape(-1))[:buffer_rows]
    )
    cot_rows = cot_buffer.reshape(adapters, capacity)
    rows_buf = jnp.take(flat_in, to_recv, axis=0).reshape(adapters, capacity, feature_cols)
    partial_pre = jnp.einsum(
        "acd,adr->acr", rows_buf, adapter_in, preferred_element_type=jnp.float32
    )
    preact = (
        lax.psum(partial_pre.astype(jnp.bfloat16), "rule").astype(jnp.float32)
        + adapter_bias[:, None, :]
    )
    sigmoid_z = jax.nn.sigmoid(preact)
    activated = preact * sigmoid_z
    reward_rows = jnp.sum(activated * adapter_out[:, None, :], axis=2)
    grad_pre = (
        cot_rows[:, :, None]
        * adapter_out[:, None, :]
        * sigmoid_z
        * (1.0 + preact * (1.0 - sigmoid_z))
    )
    grad_half = grad_pre.astype(jnp.bfloat16)
    bias_grad = jnp.sum(grad_pre, axis=1)
    out_grad = jnp.sum(cot_rows[:, :, None] * activated, axis=1)
    reward_flat = jnp.concatenate([reward_rows.reshape(-1), jnp.zeros((1,), jnp.float32)]).astype(
        jnp.bfloat16
    )
    in_grad = jnp.einsum(
        "acd,acr->adr", rows_buf, grad_half, preferred_element_type=jnp.float32
    ).astype(jnp.bfloat16)
    input_grad = jnp.einsum(
        "acr,adr->acd", grad_half, adapter_in, preferred_element_type=jnp.float32
    ).astype(jnp.bfloat16)
    grad_flat = jnp.concatenate(
        [input_grad.reshape(buffer_rows, feature_cols), jnp.zeros((1, feature_cols), jnp.bfloat16)],
        axis=0,
    )
    back_rows = jnp.take(grad_flat, to_buffer, axis=0).reshape(
        dp_size, send_cap, rule_size, feature_cols
    )
    back_reward = jnp.take(reward_flat, to_buffer, axis=0).reshape(dp_size, send_cap, rule_size)
    returned, reward_back = (
        lax.all_to_all(back_rows, "dp", split_axis=0, concat_axis=0, tiled=True),
        lax.all_to_all(back_reward, "dp", split_axis=0, concat_axis=0, tiled=True),
    )
    owner_group = lax.dynamic_slice_in_dim(owner_all, dp_index * rule_size, rule_size, 0)
    rank_group = lax.dynamic_slice_in_dim(rank_all, dp_index * rule_size, rule_size, 0)
    pair_index = (
        (owner_group * send_cap + rank_group) * rule_size + jnp.arange(rule_size)[:, None]
    ).reshape(-1)
    pair_grads = jnp.take(returned.reshape(recv_count, feature_cols), pair_index, axis=0)
    pair_grads = pair_grads.astype(jnp.float32).reshape(rule_size * rows_dev, 2, feature_cols)
    state_grad = jnp.sum(pair_grads, axis=1).astype(jnp.bfloat16)
    rewards = jnp.take(reward_back.reshape(recv_count), pair_index, axis=0).reshape(
        rule_size * rows_dev, 2
    )
    group_term = lax.dot_general(
        state_grad,
        lax.all_gather(attn_input, "rule", axis=0, tiled=True),
        (((0,), (0,)), ((), ())),
        preferred_element_type=jnp.float32,
    )
    o_proj_grad = lax.psum_scatter(
        group_term.astype(jnp.bfloat16), "dp", scatter_dimension=1, tiled=True
    )
    return (rewards, in_grad, bias_grad, out_grad, o_proj_grad)


def solution(mesh):
    placed = (
        P(("dp", "rule"), None),
        P(("dp", "rule"), None),
        P(),
        P(),
        P(),
        P("dp", "rule", None),
        P("dp", None),
        P("dp", None),
    )
    return jax.shard_map(
        local,
        mesh=mesh,
        in_specs=placed,
        out_specs=(
            P("dp", None),
            P("dp", "rule", None),
            P("dp", None),
            P("dp", None),
            P("rule", "dp"),
        ),
        check_vma=False,
    )
```

profile of v0, /device:TPU:25, one launch (start us, length us, event | category | flops | bytes accessed | tf_op | source)
XLA Modules:
  0.0 413.3 jit_solution(5841563843183169320)
XLA Ops:
  7.2 2.9 copy.44
  10.1 2.2 reshape.437
  14.8 9.4 %all-to-all-start = ((bf16[16,2,32,256]{3,1,2,0:T(2,128)(2,1)}), bf16[16,2,32,256]{3,1,2,0:T(2,128)(2,1)S(1)}, u32[]{:S(2)}, u32[]{:S(2)}) async-start(bf16[16,2,32,256]{3,1,2,0:T(2,128)(2,1)} %copy.57), calls=%async_computation | async-start | bytes 1048576 | tf_op jit(solution)/shard_map/all_to_all | solution.py:43
  24.3 3.0 reshape.439
  27.6 2.0 copy.51
  29.6 3.0 reshape.440
  32.9 6.3 %all-to-all-done = bf16[16,2,32,256]{3,1,2,0:T(2,128)(2,1)S(1)} async-done(((bf16[16,2,32,256]{3,1,2,0:T(2,128)(2,1)}), bf16[16,2,32,256]{3,1,2,0:T(2,128)(2,1)S(1)}, u32[]{:S(2)}, u32[]{:S(2)}) %all-to-all-start) | async-done | bytes 524320 | tf_op jit(solution)/shard_map/all_to_all | solution.py:43
  40.6 11.2 %all-to-all-start.1 = ((bf16[16,2,32,256]{3,1,0,2:T(2,128)(2,1)}), bf16[16,2,32,256]{3,1,0,2:T(2,128)(2,1)S(1)}, u32[]{:S(2)}, u32[]{:S(2)}) async-start(bf16[16,2,32,256]{3,1,0,2:T(2,128)(2,1)} %copy.58), calls=%async_computation.1 | async-start | bytes 1048576 | tf_op jit(solution)/shard_map/all_to_all | solution.py:42
  52.2 30.4 %scatter_custom_fusion.1 = s32[1025]{0:T(1024)S(1)} fusion(s32[8192]{0:T(1024)S(1)} %bitcast.35, s32[8192]{0:T(1024)S(1)} %reshape.505, s32[]{:T(128)} %constant.137.clone.1), kind=kCustom, calls=%fused_computation.76 | custom fusion | bytes 4104 | tf_op jit(solution)/shard_map/scatter | solution.py:63
  83.0 4.9 %gather_fusion.3 = bf16[1024,256]{1,0:T(8,128)(2,1)} fusion(bf16[1025,256]{1,0:T(8,128)(2,1)S(1)} %concatenate.10, s32[1024]{0:T(1024)S(1)} %fusion.23), kind=kCustom, calls=%fused_computation.clone | custom fusion | bytes 1052672 | tf_op jit(solution)/shard_map/jit(_take)/gather | solution.py:76
  91.5 2.7 reshape.441
  94.2 2.7 reshape.442
  97.0 30.4 %scatter_custom_fusion = s32[1025]{0:T(1024)S(1)} fusion(s32[8192]{0:T(1024)S(1)} %bitcast.34, s32[8192]{0:T(1024)S(1)} %fusion.7, s32[]{:T(128)} %constant.137.clone.1), kind=kCustom, calls=%fused_computation.78 | custom fusion | bytes 4104 | tf_op jit(solution)/shard_map/scatter | solution.py:68
  127.6 1.7 copy.61
  129.3 2.7 reshape.513
  132.0 30.4 %scatter_custom_fusion.2 = f32[1025]{0:T(1024)S(1)} fusion(s32[8192]{0:T(1024)S(1)} %bitcast.36, f32[8192]{0:T(1024)S(1)} %reshape.513, f32[]{:T(128)} %constant.147.clone.1), kind=kCustom, calls=%fused_computation.67 | custom fusion | bytes 4104 | tf_op jit(solution)/shard_map/scatter | solution.py:73
  162.5 83.6 %all-reduce.4.cloned.1.call-done = bf16[8,128,512]{2,1,0:T(8,128)(2,1)} async-done(((bf16[8,128,512]{2,1,0:T(8,128)(2,1)}), bf16[8,128,512]{2,1,0:T(8,128)(2,1)}) %all-reduce.4.cloned.1.call-update) | async-done | bytes 1048592 | tf_op jit(solution)/shard_map/psum | solution.py:81
  246.1 3.4 fusion.29
  249.5 6.8 %gather_fusion = bf16[1024]{0:T(1024)(128)(2,1)S(1)} fusion(bf16[1025]{0:T(1024)(128)(2,1)S(1)} %pad_maximum_fusion, s32[1024]{0:T(1024)S(1)} %get-tuple-element.34), kind=kCustom, calls=%fused_computation.2 | custom fusion | bytes 8192 | tf_op jit(solution)/shard_map/jit(_take)/gather | solution.py:112
  257.0 12.1 %all-to-all-start.2 = ((bf16[16,2,32]{2,1,0:T(2,128)(2,1)}), bf16[16,2,32]{2,1,0:T(2,128)(2,1)S(1)}, u32[]{:S(2)}, u32[]{:S(2)}) async-start(bf16[16,2,32]{2,1,0:T(2,128)(2,1)} %and_select_fusion.2), calls=%async_computation.2 | async-start | bytes 16384 | tf_op jit(solution)/shard_map/all_to_all | solution.py:115
  269.1 2.3 convolution_convert_fusion.4
  271.5 5.0 %gather_fusion.4 = bf16[1024,256]{1,0:T(8,128)(2,1)} fusion(bf16[1025,256]{1,0:T(8,128)(2,1)S(1)} %concatenate.12, s32[1024]{0:T(1024)S(1)} %get-tuple-element.34), kind=kCustom, calls=%fused_computation.1.clone | custom fusion | bytes 1052672 | tf_op jit(solution)/shard_map/jit(_take)/gather | solution.py:109
  276.5 2.0 broadcast_select_fusion
  278.6 7.2 %all-to-all-start.3 = ((bf16[16,2,32,256]{3,2,1,0:T(8,128)(2,1)}), bf16[16,2,32,256]{3,2,1,0:T(8,128)(2,1)S(1)}, u32[]{:S(2)}, u32[]{:S(2)}) async-start(bf16[16,2,32,256]{3,2,1,0:T(8,128)(2,1)} %bitcast.29), calls=%async_computation.3 | async-start | bytes 1048576 | tf_op jit(solution)/shard_map/all_to_all | solution.py:114
  286.5 3.5 gather_fusion.1
  290.3 10.5 %all-to-all-done.3 = bf16[16,2,32,256]{3,2,1,0:T(8,128)(2,1)S(1)} async-done(((bf16[16,2,32,256]{3,2,1,0:T(8,128)(2,1)}), bf16[16,2,32,256]{3,2,1,0:T(8,128)(2,1)S(1)}, u32[]{:S(2)}, u32[]{:S(2)}) %all-to-all-start.3) | async-done | bytes 524320 | tf_op jit(solution)/shard_map/all_to_all | solution.py:114
  300.8 1.9 gather_fusion.2
  302.8 2.0 fusion.3
  304.8 31.3 %all-gather.2.cloned.1.call-done = bf16[256,8192]{1,0:T(8,128)(2,1)} async-done(((bf16[8,8192]{1,0:T(8,128)(2,1)}), bf16[256,8192]{1,0:T(8,128)(2,1)}) %all-gather.2.cloned.1.call-update) | async-done | bytes 4194320 | tf_op jit(solution)/shard_map/all_gather | solution.py:130
  336.2 5.4 %convolution_convert_fusion = bf16[256,8192]{1,0:T(8,128)(2,1)} fusion(bf16[256,256]{1,0:T(8,128)(2,1)S(1)} %fusion.3, bf16[256,8192]{1,0:T(8,128)(2,1)} %all-gather.2.cloned.1.call-done), kind=kOutput, calls=%fused_computation.8 | convolution fusion | flops 1075838976 | bytes 8519680 | tf_op jit(solution)/shard_map/dot_general | solution.py:128
  341.6 3.8 convolution_convert_fusion.2
  346.1 60.7 %reduce-scatter.2.cloned.1.call-done = bf16[256,512]{1,0:T(8,128)(2,1)} async-done(((bf16[256,8192]{1,0:T(8,128)(2,1)}), bf16[256,512]{1,0:T(8,128)(2,1)}) %reduce-scatter.2.cloned.1.call-update) | async-done | bytes 262160 | tf_op jit(solution)/shard_map/reduce_scatter | solution.py:134
  (65 shorter events, 11.1 us)
Async XLA Ops:
  7.2 82.1 %copy-start = (bf16[8,256,512]{2,1,0:T(8,128)(2,1)S(1)}, bf16[8,256,512]{2,1,0:T(8,128)(2,1)}, u32[]{:S(2)}) copy-start(bf16[8,256,512]{2,1,0:T(8,128)(2,1)} %param.15) | copy-start | bytes 6291460
  7.2 5.8 %copy-start.1 = (bf16[8,8192]{1,0:T(8,128)(2,1)S(1)}, bf16[8,8192]{1,0:T(8,128)(2,1)}, u32[]{:S(2)}) copy-start(bf16[8,8192]{1,0:T(8,128)(2,1)} %param.10) | copy-start | bytes 393220
  14.8 12.8 %copy-start.2 = (s32[4096,2]{0,1:T(2,128)S(1)}, s32[4096,2]{0,1:T(2,128)}, u32[]{:S(2)}) copy-start(s32[4096,2]{0,1:T(2,128)} %param.13) | copy-start | bytes 98308
  14.8 24.4 %all-to-all-start = ((bf16[16,2,32,256]{3,1,2,0:T(2,128)(2,1)}), bf16[16,2,32,256]{3,1,2,0:T(2,128)(2,1)S(1)}, u32[]{:S(2)}, u32[]{:S(2)}) async-start(bf16[16,2,32,256]{3,1,2,0:T(2,128)(2,1)} %copy.57), calls=%async_computation | async-start | bytes 1048576 | tf_op jit(solution)/shard_map/all_to_all | solution.py:43
  40.6 42.1 %all-to-all-start.1 = ((bf16[16,2,32,256]{3,1,0,2:T(2,128)(2,1)}), bf16[16,2,32,256]{3,1,0,2:T(2,128)(2,1)S(1)}, u32[]{:S(2)}, u32[]{:S(2)}) async-start(bf16[16,2,32,256]{3,1,0,2:T(2,128)(2,1)} %copy.58), calls=%async_computation.1 | async-start | bytes 1048576 | tf_op jit(solution)/shard_map/all_to_all | solution.py:42
  51.8 194.3 %all-reduce.4.cloned.1.call-start = ((), (), s32[]{:S(2)}) async-start(), calls=%async_computation.5 | async-start | bytes 2097152 | tf_op jit(solution)/shard_map/psum | solution.py:81
  90.7 245.4 %all-gather.2.cloned.1.call-start = ((), (), s32[]{:S(2)}) async-start(), calls=%async_computation.6 | async-start | bytes 4325376 | tf_op jit(solution)/shard_map/all_gather | solution.py:130
  91.5 36.1 %copy-start.3 = (bf16[4096,2]{0,1:T(2,128)(2,1)S(1)}, bf16[4096,2]{0,1:T(2,128)(2,1)}, u32[]{:S(2)}) copy-start(bf16[4096,2]{0,1:T(2,128)(2,1)} %param.14) | copy-start | bytes 49156
  127.5 118.6 %copy-start.4 = (f32[8,512]{1,0:T(8,128)S(1)}, f32[8,512]{1,0:T(8,128)}, u32[]{:S(2)}) copy-start(f32[8,512]{1,0:T(8,128)} %param.16) | copy-start | bytes 49156
  127.5 118.6 %copy-start.5 = (f32[8,512]{1,0:T(8,128)S(1)}, f32[8,512]{1,0:T(8,128)}, u32[]{:S(2)}) copy-start(f32[8,512]{1,0:T(8,128)} %param.17) | copy-start | bytes 49156
  257.0 21.5 %all-to-all-start.2 = ((bf16[16,2,32]{2,1,0:T(2,128)(2,1)}), bf16[16,2,32]{2,1,0:T(2,128)(2,1)S(1)}, u32[]{:S(2)}, u32[]{:S(2)}) async-start(bf16[16,2,32]{2,1,0:T(2,128)(2,1)} %and_select_fusion.2), calls=%async_computation.2 | async-start | bytes 16384 | tf_op jit(solution)/shard_map/all_to_all | solution.py:115
  278.6 22.2 %all-to-all-start.3 = ((bf16[16,2,32,256]{3,2,1,0:T(8,128)(2,1)}), bf16[16,2,32,256]{3,2,1,0:T(8,128)(2,1)S(1)}, u32[]{:S(2)}, u32[]{:S(2)}) async-start(bf16[16,2,32,256]{3,2,1,0:T(8,128)(2,1)} %bitcast.29), calls=%async_computation.3 | async-start | bytes 1048576 | tf_op jit(solution)/shard_map/all_to_all | solution.py:114
  285.8 121.0 %reduce-scatter.2.cloned.1.call-start = ((), (), s32[]{:S(2)}) async-start(), calls=%async_computation.7 | async-start | bytes 4456448 | tf_op jit(solution)/shard_map/reduce_scatter | solution.py:134
Sparse Core Ops, SparseCore 0:
  90.8 155.2 all-reduce.3
  249.3 86.8 all-gather.1
  341.7 65.0 reduce-scatter.1
where the time goes:
time: 414 us; the launch traced here: 413 us
  waiting for transfers between devices  193 us (47%)
  local copies, waits for them, and re-layouts  142 us (34%)
  starting transfers between devices  40.5 us (10%)
  between operations  14.1 us (3%)
  matrix products  13.4 us (3%)
  other arithmetic  10.4 us (3%)
    psum x1, waiting for transfers between devices, local(): lax.psum(partial_pre.astype(jnp.bfloat16), 'rule').astype(jnp.float32)  83.6 us
    reduce_scatter x1, waiting for transfers between devices, local(): lax.psum_scatter(group_term.astype(jnp.bfloat16), 'dp', scatter_dimension...  60.7 us
    all_gather x1, waiting for transfers between devices, local(): lax.all_gather(attn_input, 'rule', axis=0, tiled=True)  31.3 us
    scatter x1, local copies, waits for them, and re-layouts, local(): to_recv = jnp.full((buffer_rows + 1,), recv_count, jnp.int32).at[pos_targ...  30.4 us
    scatter x1, local copies, waits for them, and re-layouts, local(): to_buffer = jnp.full((recv_count + 1,), buffer_rows, jnp.int32).at[recv_t...  30.4 us
    scatter x1, local copies, waits for them, and re-layouts, local(): cot_buffer = jnp.zeros((buffer_rows + 1,), jnp.float32).at[pos_target].se...  30.4 us
    all_to_all x1, starting transfers between devices, local(): lax.all_to_all(back_reward, 'dp', split_axis=0, concat_axis=0, tiled=True)  12.1 us
    all_to_all x1, starting transfers between devices, local(): lax.all_to_all(lax.all_to_all(outgoing, 'dp', split_axis=0, concat_axis=0...  11.2 us
  transfers between devices with their start and end apart: 7, of which 5 were waited for; matrix products, arithmetic and copies ran while one was open for 35% of the time, Pallas kernels for 0%

commit v1 on v0

--- a/solution.py
+++ b/solution.py
@@ -2,6 +2,29 @@
 import jax.numpy as jnp
 from jax import lax
 from jax.sharding import PartitionSpec as P
+
+
+def split_up(shard, dim, count):
+    before, after = (shard.shape[:dim], shard.shape[dim + 1 :])
+    return jnp.moveaxis(shard.reshape(*before, count, -1, *after), dim, 0)
+
+
+def laid_out(parts, dim):
+    lengths = list(parts.shape[1:])
+    lengths[dim] *= parts.shape[0]
+    return jnp.moveaxis(parts, 0, dim).reshape(lengths)
+
+
+def sent_to_each(shard, axis, split_dim, concat_dim):
+    length, index = (lax.axis_size(axis), lax.axis_index(axis))
+    blocks = split_up(shard, split_dim, length)
+    out = blocks
+    for step in range(1, length):
+        target, source = ((index + step) % length, (index - step) % length)
+        sent = lax.dynamic_index_in_dim(blocks, target, 0)
+        partner_block = lax.ppermute(sent, axis, [(i, (i + step) % length) for i in range(length)])
+        out = lax.dynamic_update_slice_in_dim(out, partner_block, source, axis=0)
+    return laid_out(out, concat_dim)
 
 
 def local(
@@ -40,11 +63,7 @@
     )
     outgoing = outgoing.reshape(dp_size, send_cap, rule_size, feature_cols)
     incoming = lax.all_to_all(
-        lax.all_to_all(outgoing, "dp", split_axis=0, concat_axis=0, tiled=True),
-        "rule",
-        split_axis=2,
-        concat_axis=2,
-        tiled=True,
+        sent_to_each(outgoing, "dp", 0, 0), "rule", split_axis=2, concat_axis=2, tiled=True
     )
     flat_in = jnp.concatenate(
         [incoming.reshape(recv_count, feature_cols), jnp.zeros((1, feature_cols), jnp.bfloat16)],

time: 414 us -> 466 us (1.13)
  the two profiles are of different devices: /device:TPU:25 before, /device:TPU:6 now
where the time goes in v1:
time: 466 us; the launch traced here: 465 us
  waiting for transfers between devices  189 us (41%)
  local copies, waits for them, and re-layouts  156 us (33%)
  starting transfers between devices  81.5 us (17%)
  between operations  14.9 us (3%)
  matrix products  13.4 us (3%)
  other arithmetic  10.4 us (2%)
    psum x1, waiting for transfers between devices, local(): lax.psum(partial_pre.astype(jnp.bfloat16), 'rule').astype(jnp.float32)  84.3 us
    reduce_scatter x1, waiting for transfers between devices, local(): lax.psum_scatter(group_term.astype(jnp.bfloat16), 'dp', scatter_dimension...  58.9 us
    ppermute x15, starting transfers between devices, sent_to_each(): lax.ppermute(sent, axis, [(i, (i + step) % length) for i in range(length)])  53.5 us
    all_gather x1, waiting for transfers between devices, local(): lax.all_gather(attn_input, 'rule', axis=0, tiled=True)  34 us
    scatter x1, local copies, waits for them, and re-layouts, local(): to_recv = jnp.full((buffer_rows + 1,), recv_count, jnp.int32).at[pos_targ...  30.4 us
    scatter x1, local copies, waits for them, and re-layouts, local(): to_buffer = jnp.full((recv_count + 1,), buffer_rows, jnp.int32).at[recv_t...  30.4 us
    scatter x1, local copies, waits for them, and re-layouts, local(): cot_buffer = jnp.zeros((buffer_rows + 1,), jnp.float32).at[pos_target].se...  30.4 us
    all_to_all x1, starting transfers between devices, local(): lax.all_to_all(sent_to_each(outgoing, 'dp', 0, 0), 'rule', split_axis=2,...  13.5 us
  transfers between devices with their start and end apart: 21, of which 4 were waited for; matrix products, arithmetic and copies ran while one was open for 34% of the time, Pallas kernels for 0%

profile of v1, /device:TPU:6, one launch (start us, length us, event | category | flops | bytes accessed | tf_op | source)
XLA Modules:
  0.0 465.1 jit_solution(11249828814003891096)
XLA Ops:
  7.4 2.9 copy.48
  15.1 3.5 collective-permute-start.1
  19.3 4.5 collective-permute-start.2
  24.4 4.8 %collective-permute-start.3 = (bf16[1,1,2,32,256]{4,2,3,1,0:T(2,128)(2,1)}, bf16[1,1,2,32,256]{4,2,3,1,0:T(2,128)(2,1)S(1)}, u32[]{:S(2)}, u32[]{:S(2)}) collective-permute-start(bf16[1,1,2,32,256]{4,2,3,1,0:T(2,128)(2,1)} %copy.86), channel_id=1, source_target_pairs={{0,128},{32,160},{64,192},{96,224},{128,256},{160,288},{192,320},{... | collective-permute-start | bytes 98312 | tf_op jit(solution)/shard_map/ppermute | solution.py:25
  31.4 3.0 reshape.500
  36.7 3.0 reshape.501
  42.1 3.7 collective-permute-start.5
  47.2 5.9 %collective-permute-start.6 = (bf16[1,1,2,32,256]{4,2,3,1,0:T(2,128)(2,1)S(1)}, bf16[1,1,2,32,256]{4,2,3,1,0:T(2,128)(2,1)S(1)}, u32[]{:S(2)}, u32[]{:S(2)}) collective-permute-start(bf16[1,1,2,32,256]{4,2,3,1,0:T(2,128)(2,1)S(1)} %copy.89), channel_id=1, source_target_pairs={{0,224},{32,256},{64,288},{96,320},{128,352},{160,384},{192,416},{... | collective-permute-start | bytes 98312 | tf_op jit(solution)/shard_map/ppermute | solution.py:25
  54.5 3.8 collective-permute-start.7
  59.8 5.4 %collective-permute-start.8 = (bf16[1,1,2,32,256]{4,2,3,1,0:T(2,128)(2,1)S(1)}, bf16[1,1,2,32,256]{4,2,3,1,0:T(2,128)(2,1)S(1)}, u32[]{:S(2)}, u32[]{:S(2)}) collective-permute-start(bf16[1,1,2,32,256]{4,2,3,1,0:T(2,128)(2,1)S(1)} %copy.91), channel_id=1, source_target_pairs={{0,288},{32,320},{64,352},{96,384},{128,416},{160,448},{192,480},{... | collective-permute-start | bytes 98312 | tf_op jit(solution)/shard_map/ppermute | solution.py:25
  65.8 3.9 collective-permute-start.9
  70.3 3.5 collective-permute-start.10
  74.5 4.0 collective-permute-start.11
  79.2 4.7 %collective-permute-start.12 = (bf16[1,1,2,32,256]{4,2,3,1,0:T(2,128)(2,1)S(1)}, bf16[1,1,2,32,256]{4,2,3,1,0:T(2,128)(2,1)S(1)}, u32[]{:S(2)}, u32[]{:S(2)}) collective-permute-start(bf16[1,1,2,32,256]{4,2,3,1,0:T(2,128)(2,1)S(1)} %copy.95), channel_id=1, source_target_pairs={{0,416},{32,448},{64,480},{96,0},{128,32},{160,64},{192,96},{224,1... | collective-permute-start | bytes 98312 | tf_op jit(solution)/shard_map/ppermute | solution.py:25
  84.5 3.2 collective-permute-start.13
  92.8 13.5 %all-to-all-start = ((bf16[16,2,32,256]{3,1,0,2:T(2,128)(2,1)}), bf16[16,2,32,256]{3,1,0,2:T(2,128)(2,1)S(1)}, u32[]{:S(2)}, u32[]{:S(2)}) async-start(bf16[16,2,32,256]{3,1,0,2:T(2,128)(2,1)} %bitcast_dynamic-update-slice_fusion), calls=%async_computation | async-start | bytes 1048576 | tf_op jit(solution)/shard_map/all_to_all | solution.py:65
  106.6 30.4 %scatter_custom_fusion.1 = s32[1025]{0:T(1024)S(1)} fusion(s32[8192]{0:T(1024)S(1)} %bitcast.70, s32[8192]{0:T(1024)S(1)} %reshape.581, s32[]{:T(128)} %constant.339.clone.1), kind=kCustom, calls=%fused_computation.115 | custom fusion | bytes 4104 | tf_op jit(solution)/shard_map/scatter | solution.py:82
  137.5 4.9 %gather_fusion.3 = bf16[1024,256]{1,0:T(8,128)(2,1)} fusion(bf16[1025,256]{1,0:T(8,128)(2,1)S(1)} %concatenate.10, s32[1024]{0:T(1024)S(1)} %fusion.30), kind=kCustom, calls=%fused_computation.clone | custom fusion | bytes 1052672 | tf_op jit(solution)/shard_map/jit(_take)/gather | solution.py:95
  151.4 30.4 %scatter_custom_fusion = s32[1025]{0:T(1024)S(1)} fusion(s32[8192]{0:T(1024)S(1)} %bitcast.69, s32[8192]{0:T(1024)S(1)} %fusion.7, s32[]{:T(128)} %constant.339.clone.1), kind=kCustom, calls=%fused_computation.117 | custom fusion | bytes 4104 | tf_op jit(solution)/shard_map/scatter | solution.py:87
  186.5 30.4 %scatter_custom_fusion.2 = f32[1025]{0:T(1024)S(1)} fusion(s32[8192]{0:T(1024)S(1)} %bitcast.71, f32[8192]{0:T(1024)S(1)} %reshape.589, f32[]{:T(128)} %constant.373.clone.1), kind=kCustom, calls=%fused_computation.106 | custom fusion | bytes 4104 | tf_op jit(solution)/shard_map/scatter | solution.py:92
  216.9 84.3 %all-reduce.4.cloned.1.call-done = bf16[8,128,512]{2,1,0:T(8,128)(2,1)} async-done(((bf16[8,128,512]{2,1,0:T(8,128)(2,1)}), bf16[8,128,512]{2,1,0:T(8,128)(2,1)}) %all-reduce.4.cloned.1.call-update) | async-done | bytes 1048592 | tf_op jit(solution)/shard_map/psum | solution.py:100
  301.3 3.4 fusion.36
  304.7 6.8 %gather_fusion = bf16[1024]{0:T(1024)(128)(2,1)S(1)} fusion(bf16[1025]{0:T(1024)(128)(2,1)S(1)} %pad_maximum_fusion, s32[1024]{0:T(1024)S(1)} %get-tuple-element.44), kind=kCustom, calls=%fused_computation.2 | custom fusion | bytes 8192 | tf_op jit(solution)/shard_map/jit(_take)/gather | solution.py:131
  312.2 6.8 %all-to-all-start.1 = ((bf16[16,2,32]{2,1,0:T(2,128)(2,1)}), bf16[16,2,32]{2,1,0:T(2,128)(2,1)S(1)}, u32[]{:S(2)}, u32[]{:S(2)}) async-start(bf16[16,2,32]{2,1,0:T(2,128)(2,1)} %and_select_fusion.2), calls=%async_computation.1 | async-start | bytes 16384 | tf_op jit(solution)/shard_map/all_to_all | solution.py:134
  321.4 5.0 %gather_fusion.4 = bf16[1024,256]{1,0:T(8,128)(2,1)} fusion(bf16[1025,256]{1,0:T(8,128)(2,1)S(1)} %concatenate.12, s32[1024]{0:T(1024)S(1)} %get-tuple-element.44), kind=kCustom, calls=%fused_computation.1.clone | custom fusion | bytes 1052672 | tf_op jit(solution)/shard_map/jit(_take)/gather | solution.py:128
  328.4 7.2 %all-to-all-start.2 = ((bf16[16,2,32,256]{3,2,1,0:T(8,128)(2,1)}), bf16[16,2,32,256]{3,2,1,0:T(8,128)(2,1)S(1)}, u32[]{:S(2)}, u32[]{:S(2)}) async-start(bf16[16,2,32,256]{3,2,1,0:T(8,128)(2,1)} %bitcast.65), calls=%async_computation.2 | async-start | bytes 1048576 | tf_op jit(solution)/shard_map/all_to_all | solution.py:133
  336.4 3.5 gather_fusion.1
  340.1 11.5 %all-to-all-done.2 = bf16[16,2,32,256]{3,2,1,0:T(8,128)(2,1)S(1)} async-done(((bf16[16,2,32,256]{3,2,1,0:T(8,128)(2,1)}), bf16[16,2,32,256]{3,2,1,0:T(8,128)(2,1)S(1)}, u32[]{:S(2)}, u32[]{:S(2)}) %all-to-all-start.2) | async-done | bytes 524320 | tf_op jit(solution)/shard_map/all_to_all | solution.py:133
  355.7 34.0 %all-gather.2.cloned.1.call-done = bf16[256,8192]{1,0:T(8,128)(2,1)} async-done(((bf16[8,8192]{1,0:T(8,128)(2,1)}), bf16[256,8192]{1,0:T(8,128)(2,1)}) %all-gather.2.cloned.1.call-update) | async-done | bytes 4194320 | tf_op jit(solution)/shard_map/all_gather | solution.py:149
  389.7 5.4 %convolution_convert_fusion = bf16[256,8192]{1,0:T(8,128)(2,1)} fusion(bf16[256,256]{1,0:T(8,128)(2,1)S(1)} %fusion.3, bf16[256,8192]{1,0:T(8,128)(2,1)} %all-gather.2.cloned.1.call-done), kind=kOutput, calls=%fused_computation.8 | convolution fusion | flops 1075838976 | bytes 8519680 | tf_op jit(solution)/shard_map/dot_general | solution.py:147
  395.2 3.8 convolution_convert_fusion.2
  399.6 58.9 %reduce-scatter.2.cloned.1.call-done = bf16[256,512]{1,0:T(8,128)(2,1)} async-done(((bf16[256,8192]{1,0:T(8,128)(2,1)}), bf16[256,512]{1,0:T(8,128)(2,1)}) %reduce-scatter.2.cloned.1.call-update) | async-done | bytes 262160 | tf_op jit(solution)/shard_map/reduce_scatter | solution.py:153
  (123 shorter events, 49.9 us)
Async XLA Ops:
  7.2 136.5 %copy-start = (bf16[8,256,512]{2,1,0:T(8,128)(2,1)S(1)}, bf16[8,256,512]{2,1,0:T(8,128)(2,1)}, u32[]{:S(2)}) copy-start(bf16[8,256,512]{2,1,0:T(8,128)(2,1)} %param.15) | copy-start | bytes 6291460
  7.4 5.8 %copy-start.1 = (bf16[8,8192]{1,0:T(8,128)(2,1)S(1)}, bf16[8,8192]{1,0:T(8,128)(2,1)}, u32[]{:S(2)}) copy-start(bf16[8,8192]{1,0:T(8,128)(2,1)} %param.10) | copy-start | bytes 393220
  13.7 21.1 %copy-start.2 = (s32[4096,2]{0,1:T(2,128)S(1)}, s32[4096,2]{0,1:T(2,128)}, u32[]{:S(2)}) copy-start(s32[4096,2]{0,1:T(2,128)} %param.13) | copy-start | bytes 98308
  14.5 27.6 %collective-permute-start = (bf16[1,1,2,32,256]{4,2,3,1,0:T(2,128)(2,1)}, bf16[1,1,2,32,256]{4,2,3,1,0:T(2,128)(2,1)}, u32[]{:S(2)}, u32[]{:S(2)}) collective-permute-start(bf16[1,1,2,32,256]{4,2,3,1,0:T(2,128)(2,1)} %copy.83), channel_id=1, source_target_pairs={{0,32},{32,64},{64,96},{96,128},{128,160},{160,192},{192,224},{224... | collective-permute-start | bytes 98312 | tf_op jit(solution)/shard_map/ppermute | solution.py:25
  15.1 32.0 %collective-permute-start.1 = (bf16[1,1,2,32,256]{4,2,3,1,0:T(2,128)(2,1)}, bf16[1,1,2,32,256]{4,2,3,1,0:T(2,128)(2,1)}, u32[]{:S(2)}, u32[]{:S(2)}) collective-permute-start(bf16[1,1,2,32,256]{4,2,3,1,0:T(2,128)(2,1)} %copy.84), channel_id=1, source_target_pairs={{0,64},{32,96},{64,128},{96,160},{128,192},{160,224},{192,256},{22... | collective-permute-start | bytes 98312 | tf_op jit(solution)/shard_map/ppermute | solution.py:25
  19.3 35.3 %collective-permute-start.2 = (bf16[1,1,2,32,256]{4,2,3,1,0:T(2,128)(2,1)}, bf16[1,1,2,32,256]{4,2,3,1,0:T(2,128)(2,1)}, u32[]{:S(2)}, u32[]{:S(2)}) collective-permute-start(bf16[1,1,2,32,256]{4,2,3,1,0:T(2,128)(2,1)} %copy.85), channel_id=1, source_target_pairs={{0,96},{32,128},{64,160},{96,192},{128,224},{160,256},{192,288},{2... | collective-permute-start | bytes 98312 | tf_op jit(solution)/shard_map/ppermute | solution.py:25
  24.4 35.4 %collective-permute-start.3 = (bf16[1,1,2,32,256]{4,2,3,1,0:T(2,128)(2,1)}, bf16[1,1,2,32,256]{4,2,3,1,0:T(2,128)(2,1)S(1)}, u32[]{:S(2)}, u32[]{:S(2)}) collective-permute-start(bf16[1,1,2,32,256]{4,2,3,1,0:T(2,128)(2,1)} %copy.86), channel_id=1, source_target_pairs={{0,128},{32,160},{64,192},{96,224},{128,256},{160,288},{192,320},{... | collective-permute-start | bytes 98312 | tf_op jit(solution)/shard_map/ppermute | solution.py:25
  29.2 36.5 %collective-permute-start.4 = (bf16[1,1,2,32,256]{4,2,3,1,0:T(2,128)(2,1)S(1)}, bf16[1,1,2,32,256]{4,2,3,1,0:T(2,128)(2,1)S(1)}, u32[]{:S(2)}, u32[]{:S(2)}) collective-permute-start(bf16[1,1,2,32,256]{4,2,3,1,0:T(2,128)(2,1)S(1)} %copy.87), channel_id=1, source_target_pairs={{0,160},{32,192},{64,224},{96,256},{128,288},{160,320},{192,352},{... | collective-permute-start | bytes 98312 | tf_op jit(solution)/shard_map/ppermute | solution.py:25
  42.1 28.2 %collective-permute-start.5 = (bf16[1,1,2,32,256]{4,2,3,1,0:T(2,128)(2,1)S(1)}, bf16[1,1,2,32,256]{4,2,3,1,0:T(2,128)(2,1)S(1)}, u32[]{:S(2)}, u32[]{:S(2)}) collective-permute-start(bf16[1,1,2,32,256]{4,2,3,1,0:T(2,128)(2,1)S(1)} %copy.88), channel_id=1, source_target_pairs={{0,192},{32,224},{64,256},{96,288},{128,320},{160,352},{192,384},{... | collective-permute-start | bytes 98312 | tf_op jit(solution)/shard_map/ppermute | solution.py:25
  47.2 27.4 %collective-permute-start.6 = (bf16[1,1,2,32,256]{4,2,3,1,0:T(2,128)(2,1)S(1)}, bf16[1,1,2,32,256]{4,2,3,1,0:T(2,128)(2,1)S(1)}, u32[]{:S(2)}, u32[]{:S(2)}) collective-permute-start(bf16[1,1,2,32,256]{4,2,3,1,0:T(2,128)(2,1)S(1)} %copy.89), channel_id=1, source_target_pairs={{0,224},{32,256},{64,288},{96,320},{128,352},{160,384},{192,416},{... | collective-permute-start | bytes 98312 | tf_op jit(solution)/shard_map/ppermute | solution.py:25
  54.5 24.6 %collective-permute-start.7 = (bf16[1,1,2,32,256]{4,2,3,1,0:T(2,128)(2,1)S(1)}, bf16[1,1,2,32,256]{4,2,3,1,0:T(2,128)(2,1)S(1)}, u32[]{:S(2)}, u32[]{:S(2)}) collective-permute-start(bf16[1,1,2,32,256]{4,2,3,1,0:T(2,128)(2,1)S(1)} %copy.90), channel_id=1, source_target_pairs={{0,256},{32,288},{64,320},{96,352},{128,384},{160,416},{192,448},{... | collective-permute-start | bytes 98312 | tf_op jit(solution)/shard_map/ppermute | solution.py:25
  59.8 24.8 %collective-permute-start.8 = (bf16[1,1,2,32,256]{4,2,3,1,0:T(2,128)(2,1)S(1)}, bf16[1,1,2,32,256]{4,2,3,1,0:T(2,128)(2,1)S(1)}, u32[]{:S(2)}, u32[]{:S(2)}) collective-permute-start(bf16[1,1,2,32,256]{4,2,3,1,0:T(2,128)(2,1)S(1)} %copy.91), channel_id=1, source_target_pairs={{0,288},{32,320},{64,352},{96,384},{128,416},{160,448},{192,480},{... | collective-permute-start | bytes 98312 | tf_op jit(solution)/shard_map/ppermute | solution.py:25
  65.8 22.6 %collective-permute-start.9 = (bf16[1,1,2,32,256]{4,2,3,1,0:T(2,128)(2,1)S(1)}, bf16[1,1,2,32,256]{4,2,3,1,0:T(2,128)(2,1)S(1)}, u32[]{:S(2)}, u32[]{:S(2)}) collective-permute-start(bf16[1,1,2,32,256]{4,2,3,1,0:T(2,128)(2,1)S(1)} %copy.92), channel_id=1, source_target_pairs={{0,320},{32,352},{64,384},{96,416},{128,448},{160,480},{192,0},{22... | collective-permute-start | bytes 98312 | tf_op jit(solution)/shard_map/ppermute | solution.py:25
  70.3 19.3 %collective-permute-start.10 = (bf16[1,1,2,32,256]{4,2,3,1,0:T(2,128)(2,1)S(1)}, bf16[1,1,2,32,256]{4,2,3,1,0:T(2,128)(2,1)S(1)}, u32[]{:S(2)}, u32[]{:S(2)}) collective-permute-start(bf16[1,1,2,32,256]{4,2,3,1,0:T(2,128)(2,1)S(1)} %copy.93), channel_id=1, source_target_pairs={{0,352},{32,384},{64,416},{96,448},{128,480},{160,0},{192,32},{224... | collective-permute-start | bytes 98312 | tf_op jit(solution)/shard_map/ppermute | solution.py:25
  74.5 15.7 %collective-permute-start.11 = (bf16[1,1,2,32,256]{4,2,3,1,0:T(2,128)(2,1)S(1)}, bf16[1,1,2,32,256]{4,2,3,1,0:T(2,128)(2,1)S(1)}, u32[]{:S(2)}, u32[]{:S(2)}) collective-permute-start(bf16[1,1,2,32,256]{4,2,3,1,0:T(2,128)(2,1)S(1)} %copy.94), channel_id=1, source_target_pairs={{0,384},{32,416},{64,448},{96,480},{128,0},{160,32},{192,64},{224,... | collective-permute-start | bytes 98312 | tf_op jit(solution)/shard_map/ppermute | solution.py:25
  79.2 11.7 %collective-permute-start.12 = (bf16[1,1,2,32,256]{4,2,3,1,0:T(2,128)(2,1)S(1)}, bf16[1,1,2,32,256]{4,2,3,1,0:T(2,128)(2,1)S(1)}, u32[]{:S(2)}, u32[]{:S(2)}) collective-permute-start(bf16[1,1,2,32,256]{4,2,3,1,0:T(2,128)(2,1)S(1)} %copy.95), channel_id=1, source_target_pairs={{0,416},{32,448},{64,480},{96,0},{128,32},{160,64},{192,96},{224,1... | collective-permute-start | bytes 98312 | tf_op jit(solution)/shard_map/ppermute | solution.py:25
  84.5 7.0 %collective-permute-start.13 = (bf16[1,1,2,32,256]{4,2,3,1,0:T(2,128)(2,1)S(1)}, bf16[1,1,2,32,256]{4,2,3,1,0:T(2,128)(2,1)S(1)}, u32[]{:S(2)}, u32[]{:S(2)}) collective-permute-start(bf16[1,1,2,32,256]{4,2,3,1,0:T(2,128)(2,1)S(1)} %copy.96), channel_id=1, source_target_pairs={{0,448},{32,480},{64,0},{96,32},{128,64},{160,96},{192,128},{224,1... | collective-permute-start | bytes 98312 | tf_op jit(solution)/shard_map/ppermute | solution.py:25
  88.4 3.8 collective-permute-start.14
  92.8 44.3 %all-to-all-start = ((bf16[16,2,32,256]{3,1,0,2:T(2,128)(2,1)}), bf16[16,2,32,256]{3,1,0,2:T(2,128)(2,1)S(1)}, u32[]{:S(2)}, u32[]{:S(2)}) async-start(bf16[16,2,32,256]{3,1,0,2:T(2,128)(2,1)} %bitcast_dynamic-update-slice_fusion), calls=%async_computation | async-start | bytes 1048576 | tf_op jit(solution)/shard_map/all_to_all | solution.py:65
  106.3 195.0 %all-reduce.4.cloned.1.call-start = ((), (), s32[]{:S(2)}) async-start(), calls=%async_computation.4 | async-start | bytes 2097152 | tf_op jit(solution)/shard_map/psum | solution.py:100
  145.1 244.6 %all-gather.2.cloned.1.call-start = ((), (), s32[]{:S(2)}) async-start(), calls=%async_computation.5 | async-start | bytes 4325376 | tf_op jit(solution)/shard_map/all_gather | solution.py:149
  145.9 36.1 %copy-start.3 = (bf16[4096,2]{0,1:T(2,128)(2,1)S(1)}, bf16[4096,2]{0,1:T(2,128)(2,1)}, u32[]{:S(2)}) copy-start(bf16[4096,2]{0,1:T(2,128)(2,1)} %param.14) | copy-start | bytes 49156
  182.0 119.3 %copy-start.4 = (f32[8,512]{1,0:T(8,128)S(1)}, f32[8,512]{1,0:T(8,128)}, u32[]{:S(2)}) copy-start(f32[8,512]{1,0:T(8,128)} %param.16) | copy-start | bytes 49156
  182.0 119.3 %copy-start.5 = (f32[8,512]{1,0:T(8,128)S(1)}, f32[8,512]{1,0:T(8,128)}, u32[]{:S(2)}) copy-start(f32[8,512]{1,0:T(8,128)} %param.17) | copy-start | bytes 49156
  312.2 16.3 %all-to-all-start.1 = ((bf16[16,2,32]{2,1,0:T(2,128)(2,1)}), bf16[16,2,32]{2,1,0:T(2,128)(2,1)S(1)}, u32[]{:S(2)}, u32[]{:S(2)}) async-start(bf16[16,2,32]{2,1,0:T(2,128)(2,1)} %and_select_fusion.2), calls=%async_computation.1 | async-start | bytes 16384 | tf_op jit(solution)/shard_map/all_to_all | solution.py:134
  328.4 23.2 %all-to-all-start.2 = ((bf16[16,2,32,256]{3,2,1,0:T(8,128)(2,1)}), bf16[16,2,32,256]{3,2,1,0:T(8,128)(2,1)S(1)}, u32[]{:S(2)}, u32[]{:S(2)}) async-start(bf16[16,2,32,256]{3,2,1,0:T(8,128)(2,1)} %bitcast.65), calls=%async_computation.2 | async-start | bytes 1048576 | tf_op jit(solution)/shard_map/all_to_all | solution.py:133
  335.7 122.9 %reduce-scatter.2.cloned.1.call-start = ((), (), s32[]{:S(2)}) async-start(), calls=%async_computation.6 | async-start | bytes 4456448 | tf_op jit(solution)/shard_map/reduce_scatter | solution.py:153
Sparse Core Ops, SparseCore 0:
  145.3 155.9 all-reduce.3
  304.4 85.2 all-gather.1
  395.3 63.2 reduce-scatter.1
